TPU v7x, 256 devices: a whole 4x4x8 slice. The times are simulated.
256 devices in a mesh: sec: 16 (over z, core), op: 16 (over x, y).
Axes of the slice: x: 4, y: 4, z: 8, core: 2. Of those that a mesh axis runs over, the one named last changes fastest.
Arguments:
- theta: float32 [32, 512, 512], P('sec', 'op'), may hold values from -6 to 6
- counts: int32 [32], P('sec'), may hold values from 256 to 512, as said below
- pair_source: int32 [256], P('sec'), may hold values from 0 to 1
- pair_target: int32 [256], P('sec'), may hold values from 0 to 31
- left_ops: float32 [1024, 512, 512], P(('sec', 'op')), may hold values from -0.25 to 0.25
- right_ops: float32 [1024, 512, 512], P(('sec', 'op')), may hold values from -0.25 to 0.25
Outputs:
- cheb_last: float32 [32, 512, 512], P('sec', 'op')
- cheb_prev: float32 [32, 512, 512], P('sec', 'op')
Inputs may be any that keep to these rules, and one draw needn't show every extreme that they name: `counts`: every sector has between 256 and 512 live states; some sector has exactly 512 and some exactly 256.
All inputs are finite; a program needn't handle non-finite values.
Results may differ from a plain program's by a relative error of at most 0.0001.
Values sent between devices are 32-bit elements; how exact they have to be, the bound alone decides.
A program may use at most 64 MiB of HBM per device.

v0:
```python
import math
import jax
import jax.numpy as jnp
from jax import lax
from jax.sharding import PartitionSpec as P

STEPS = 3


def per_device(theta, counts, pair_source, pair_target, left_ops, right_ops):
    op_count = lax.axis_size("op")
    op_place = lax.axis_index("op")
    sec_place = lax.axis_index("sec")
    sec_local = theta.shape[0]
    row_count = theta.shape[1]
    order_size = theta.shape[2]
    pairs_local = left_ops.shape[0]
    group_blocks = pair_target.shape[0]
    sectors_all = sec_local * lax.axis_size("sec")
    factor = 0.5 / math.sqrt(group_blocks * pairs_local / sec_local)
    highest = lax.Precision.HIGHEST
    my_source = lax.dynamic_index_in_dim(pair_source, op_place, 0, keepdims=False)
    row_numbers = op_place * row_count + jnp.arange(row_count, dtype=jnp.int32)
    row_alive = row_numbers[None, :] < counts[:, None]
    column_alive = jnp.arange(order_size, dtype=jnp.int32)[None, :] < counts[:, None]
    live_mask = (row_alive[:, :, None] & column_alive[:, None, :]).astype(jnp.float32)
    target_hot = (pair_target[None, :] == jnp.arange(sectors_all, dtype=jnp.int32)[:, None]).astype(
        jnp.float32
    )

    def hamiltonian(iterate):
        gathered = lax.all_gather(iterate, "op", axis=1, tiled=True)
        chosen = lax.dynamic_index_in_dim(gathered, my_source, 0, keepdims=False)
        left_product = jnp.einsum("pmr,rn->pmn", left_ops, chosen, precision=highest)
        block_term = jnp.einsum("pmk,pnk->mn", left_product, right_ops, precision=highest)
        split_rows = block_term.reshape(op_count, row_count, order_size)
        block_rows = lax.all_to_all(split_rows, "op", split_axis=0, concat_axis=0, tiled=True)
        flat_rows = block_rows.reshape(group_blocks, row_count * order_size)
        sector_sums = jnp.dot(
            target_hot, flat_rows, precision=highest, preferred_element_type=jnp.float32
        )
        sector_sums = sector_sums.reshape(sectors_all, row_count, order_size)
        whole_sums = lax.psum(sector_sums, "sec")
        own_sums = lax.dynamic_slice_in_dim(whole_sums, sec_place * sec_local, sec_local, 0)
        return factor * own_sums * live_mask

    previous = theta * live_mask
    current = hamiltonian(previous)
    for step_number in range(STEPS - 1):
        following = 2.0 * hamiltonian(current) - previous
        previous, current = (current, following)
    return (current, previous)


def solution(mesh):
    in_specs = (
        P("sec", "op", None),
        P("sec"),
        P("sec"),
        P("sec"),
        P(("sec", "op"), None, None),
        P(("sec", "op"), None, None),
    )
    out_specs = (P("sec", "op", None), P("sec", "op", None))
    return jax.shard_map(
        per_device, mesh=mesh, in_specs=in_specs, out_specs=out_specs, check_vma=False
    )
```

profile of v0, /device:TPU:1, one launch (start us, length us, event | category | flops | bytes accessed | tf_op | source)
XLA Modules:
  0.0 675.0 jit_solution(8471230393268469698)
XLA Ops:
  7.2 0.7 iota_compare_fusion.1
  8.0 0.7 broadcast_compare_fusion
  8.7 1.7 and_select_fusion.3
  10.5 1.2 dynamic_slice.23
  13.7 50.3 %all-gather.4.cloned.1.call-done = f32[2,512,512]{2,0,1:T(2,128)} async-done(((f32[2,32,512]{2,0,1:T(2,128)}), f32[2,512,512]{2,0,1:T(2,128)}) %all-gather.4.cloned.1.call-update) | async-done | bytes 2097168 | tf_op jit(solution)/shard_map/all_gather | solution.py:32
  63.9 2.5 constant_dynamic-slice_fusion.2
  66.4 1.3 copy.18
  67.8 10.3 %fusion.19 = f32[512,4,512]{2,0,1:T(8,128)S(1)} fusion(f32[4,512,512]{2,1,0:T(8,128)} %param.10, f32[1,512,512]{1,2,0:T(8,128)S(1)} %copy.18), kind=kOutput, calls=%fused_computation.19 | convolution fusion | flops 6442450944 | bytes 9437184 | tf_op jit(solution)/shard_map/pmr,rn->pmn/dot_general | solution.py:34
  78.1 13.9 %fusion.4 = f32[512,512,1]{1,0,2:T(8,128)S(1)} fusion(f32[4,512,512]{2,1,0:T(8,128)S(1)} %copy-done, f32[512,4,512]{2,0,1:T(8,128)S(1)} %fusion.19), kind=kOutput, calls=%fused_computation.4 | convolution fusion | flops 6442450944 | bytes 9437184 | tf_op jit(solution)/shard_map/pmk,pnk->mn/dot_general | solution.py:35
  92.0 19.3 %all_to_all.15 = f32[16,32,512]{2,1,0:T(8,128)S(1)} all-to-all(f32[16,32,512]{2,1,0:T(8,128)S(1)} %bitcast.75), channel_id=1, replica_groups=mesh['sec'=16,'op'=16] {'op'}, dimensions={0} | all-to-all | bytes 2097152 | tf_op jit(solution)/shard_map/all_to_all | solution.py:37
  111.3 2.9 fusion.12
  114.2 115.1 %all-reduce.4.cloned.1.call-done = f32[32,32,512]{2,0,1:T(8,128)} async-done(((f32[32,32,512]{2,0,1:T(8,128)}), f32[32,32,512]{2,0,1:T(8,128)}) %all-reduce.4.cloned.1.call-update) | async-done | bytes 2097168 | tf_op jit(solution)/shard_map/psum | solution.py:43
  229.4 1.8 and_select_fusion.2
  231.3 50.7 %all-gather.6.cloned.1.call-done = f32[2,512,512]{2,0,1:T(2,128)} async-done(((f32[2,32,512]{2,0,1:T(2,128)}), f32[2,512,512]{2,0,1:T(2,128)}) %all-gather.6.cloned.1.call-update) | async-done | bytes 2097168 | tf_op jit(solution)/shard_map/all_gather | solution.py:32
  282.0 2.5 constant_dynamic-slice_fusion.1
  284.5 1.3 copy.21
  285.8 10.3 %fusion.17 = f32[512,4,512]{2,0,1:T(8,128)S(1)} fusion(f32[4,512,512]{2,1,0:T(8,128)} %param.10, f32[1,512,512]{1,2,0:T(8,128)S(1)} %copy.21), kind=kOutput, calls=%fused_computation.17 | convolution fusion | flops 6442450944 | bytes 9437184 | tf_op jit(solution)/shard_map/pmr,rn->pmn/dot_general | solution.py:34
  296.1 13.7 %fusion.2 = f32[512,512,1]{1,0,2:T(8,128)S(1)} fusion(f32[4,512,512]{2,1,0:T(8,128)S(1)} %copy-done.1, f32[512,4,512]{2,0,1:T(8,128)S(1)} %fusion.17), kind=kOutput, calls=%fused_computation.2 | convolution fusion | flops 6442450944 | bytes 9437184 | tf_op jit(solution)/shard_map/pmk,pnk->mn/dot_general | solution.py:35
  309.9 19.4 %all_to_all.16 = f32[16,32,512]{2,1,0:T(8,128)S(1)} all-to-all(f32[16,32,512]{2,1,0:T(8,128)S(1)} %bitcast.76), channel_id=1, replica_groups=mesh['sec'=16,'op'=16] {'op'}, dimensions={0} | all-to-all | bytes 2097152 | tf_op jit(solution)/shard_map/all_to_all | solution.py:37
  329.2 2.9 fusion.9
  332.2 115.3 %all-reduce.6.cloned.1.call-done = f32[32,32,512]{2,0,1:T(8,128)} async-done(((f32[32,32,512]{2,0,1:T(8,128)}), f32[32,32,512]{2,0,1:T(8,128)}) %all-reduce.6.cloned.1.call-update) | async-done | bytes 2097168 | tf_op jit(solution)/shard_map/psum | solution.py:43
  447.5 1.9 fusion.22
  449.5 50.4 %all-gather.8.cloned.1.call-done = f32[2,512,512]{2,0,1:T(2,128)} async-done(((f32[2,32,512]{2,0,1:T(2,128)}), f32[2,512,512]{2,0,1:T(2,128)}) %all-gather.8.cloned.1.call-update) | async-done | bytes 2097168 | tf_op jit(solution)/shard_map/all_gather | solution.py:32
  500.0 2.5 constant_dynamic-slice_fusion
  502.5 1.3 copy.24
  503.8 10.3 %fusion.15 = f32[512,4,512]{2,0,1:T(8,128)S(1)} fusion(f32[4,512,512]{2,1,0:T(8,128)} %param.10, f32[1,512,512]{1,2,0:T(8,128)S(1)} %copy.24), kind=kOutput, calls=%fused_computation.15 | convolution fusion | flops 6442450944 | bytes 9437184 | tf_op jit(solution)/shard_map/pmr,rn->pmn/dot_general | solution.py:34
  514.1 13.8 %fusion = f32[512,512,1]{1,0,2:T(8,128)S(1)} fusion(f32[4,512,512]{2,1,0:T(8,128)S(1)} %copy-done.2, f32[512,4,512]{2,0,1:T(8,128)S(1)} %fusion.15), kind=kOutput, calls=%fused_computation | convolution fusion | flops 6442450944 | bytes 9437184 | tf_op jit(solution)/shard_map/pmk,pnk->mn/dot_general | solution.py:35
  528.0 19.4 %all_to_all.17 = f32[16,32,512]{2,1,0:T(8,128)S(1)} all-to-all(f32[16,32,512]{2,1,0:T(8,128)S(1)} %bitcast.77), channel_id=1, replica_groups=mesh['sec'=16,'op'=16] {'op'}, dimensions={0} | all-to-all | bytes 2097152 | tf_op jit(solution)/shard_map/all_to_all | solution.py:37
  547.4 2.9 fusion.6
  550.3 0.7 copy.28
  551.0 114.5 %all-reduce.8.cloned.1.call-done = f32[32,32,512]{2,0,1:T(8,128)} async-done(((f32[32,32,512]{2,0,1:T(8,128)}), f32[32,32,512]{2,0,1:T(8,128)}) %all-reduce.8.cloned.1.call-update) | async-done | bytes 2097168 | tf_op jit(solution)/shard_map/psum | solution.py:43
  665.5 1.4 fusion.24
  (26 shorter events, 1.1 us)
Async XLA Ops:
  7.2 56.8 %all-gather.4.cloned.1.call-start = ((), (), s32[]{:S(2)}) async-start(), calls=%async_computation.3 | async-start | bytes 2228224 | tf_op jit(solution)/shard_map/all_gather | solution.py:32
  10.4 219.0 %all-reduce.4.cloned.1.call-start = ((), (), s32[]{:S(2)}) async-start(), calls=%async_computation.4 | async-start | bytes 4194304 | tf_op jit(solution)/shard_map/psum | solution.py:43
  67.8 10.3 %copy-start = (f32[4,512,512]{2,1,0:T(8,128)S(1)}, f32[4,512,512]{2,1,0:T(8,128)}, u32[]{:S(2)}) copy-start(f32[4,512,512]{2,1,0:T(8,128)} %param.11) | copy-start | bytes 12582916
  78.1 33.2 %copy-start.5 = (s32[16]{0:T(128)S(1)}, s32[16]{0:T(128)}, u32[]{:S(2)}) copy-start(s32[16]{0:T(128)} %param.9) | copy-start | bytes 196
  114.2 167.8 %all-gather.6.cloned.1.call-start = ((), (), s32[]{:S(2)}) async-start(), calls=%async_computation.5 | async-start | bytes 2228224 | tf_op jit(solution)/shard_map/all_gather | solution.py:32
  231.3 216.3 %all-reduce.6.cloned.1.call-start = ((), (), s32[]{:S(2)}) async-start(), calls=%async_computation.6 | async-start | bytes 4194304 | tf_op jit(solution)/shard_map/psum | solution.py:43
  285.8 10.3 %copy-start.1 = (f32[4,512,512]{2,1,0:T(8,128)S(1)}, f32[4,512,512]{2,1,0:T(8,128)}, u32[]{:S(2)}) copy-start(f32[4,512,512]{2,1,0:T(8,128)} %param.11) | copy-start | bytes 12582916
  309.8 137.7 %copy-start.4 = (f32[2,32,512]{2,1,0:T(8,128)S(1)}, f32[2,32,512]{2,1,0:T(8,128)}, u32[]{:S(2)}) copy-start(f32[2,32,512]{2,1,0:T(8,128)} %param.6) | copy-start | bytes 393220
  332.2 167.8 %all-gather.8.cloned.1.call-start = ((), (), s32[]{:S(2)}) async-start(), calls=%async_computation.7 | async-start | bytes 2228224 | tf_op jit(solution)/shard_map/all_gather | solution.py:32
  449.5 216.0 %all-reduce.8.cloned.1.call-start = ((), (), s32[]{:S(2)}) async-start(), calls=%async_computation.8 | async-start | bytes 4194304 | tf_op jit(solution)/shard_map/psum | solution.py:43
  503.8 10.4 %copy-start.2 = (f32[4,512,512]{2,1,0:T(8,128)S(1)}, f32[4,512,512]{2,1,0:T(8,128)}, u32[]{:S(2)}) copy-start(f32[4,512,512]{2,1,0:T(8,128)} %param.11) | copy-start | bytes 12582916
  528.0 22.3 %copy-start.3 = (f32[2,32,512]{2,0,1:T(2,128)S(1)}, f32[2,32,512]{2,0,1:T(2,128)}, u32[]{:S(2)}) copy-start(f32[2,32,512]{2,0,1:T(2,128)} %fusion.22) | copy-start | bytes 393220
Sparse Core Ops, SparseCore 0:
  11.0 52.8 all-gather.3
  114.3 115.0 all-reduce.3
  232.4 49.5 all-gather.5
  332.3 115.2 all-reduce.5
  450.4 49.5 all-gather.7
  550.4 115.0 all-reduce.7
where the time goes:
time: 680 us; the launch traced here: 675 us
  waiting for transfers between devices  496 us (73%)
  matrix products  81 us (12%)
  blocking collectives  58 us (9%)
  between operations  16.7 us (2%)
  local copies, waits for them, and re-layouts  14 us (2%)
  other arithmetic  8.39 us (1%)
    psum x3, waiting for transfers between devices, hamiltonian(): whole_sums = lax.psum(sector_sums, 'sec')  345 us
    all_gather x3, waiting for transfers between devices, hamiltonian(): gathered = lax.all_gather(iterate, 'op', axis=1, tiled=True)  151 us
    all_to_all x3, blocking collectives, hamiltonian(): lax.all_to_all(split_rows, 'op', split_axis=0, concat_axis=0, tiled=True)  58 us
    dot_general x3, matrix products, hamiltonian(): jnp.einsum('pmk,pnk->mn', left_product, right_ops, precision=highest)  41.5 us
    dot_general x3, matrix products, hamiltonian(): jnp.einsum('pmr,rn->pmn', left_ops, chosen, precision=highest)  30.9 us
  transfers between devices with their start and end apart: 6, of which 6 were waited for; matrix products, arithmetic and copies ran while one was open for 0% of the time, Pallas kernels for 0%

commit v1 on v0

--- a/solution.py
+++ b/solution.py
@@ -40,7 +40,11 @@
             target_hot, flat_rows, precision=highest, preferred_element_type=jnp.float32
         )
         sector_sums = sector_sums.reshape(sectors_all, row_count, order_size)
-        whole_sums = lax.psum(sector_sums, "sec")
+        whole_sums = sector_sums
+        for hop in (1, 2, 4, 8):
+            whole_sums = whole_sums + lax.ppermute(
+                whole_sums, "sec", [(dev, dev ^ hop) for dev in range(16)]
+            )
         own_sums = lax.dynamic_slice_in_dim(whole_sums, sec_place * sec_local, sec_local, 0)
         return factor * own_sums * live_mask
 

time: 680 us -> 1050 us (1.54)
  waiting for transfers between devices: 496 us -> 830 us
  starting transfers between devices: 0.25 us -> 40.9 us
    ppermute x0 -> x12, waiting for transfers between devices: none -> 690 us  [hamiltonian(): lax.ppermute(whole_sums, 'sec', [(dev, dev ^ hop) for dev in range(16)])]
    psum x3 -> x0, waiting for transfers between devices: 345 us -> none  [hamiltonian(): whole_sums = lax.psum(sector_sums, 'sec')]
    ppermute x0 -> x12, starting transfers between devices: none -> 40.7 us  [hamiltonian(): lax.ppermute(whole_sums, 'sec', [(dev, dev ^ hop) for dev in range(16)])]
    all_gather x3, waiting for transfers between devices: 151 us -> 140 us  [hamiltonian(): gathered = lax.all_gather(iterate, 'op', axis=1, tiled=True)]
  transfers between devices with their start and end apart: 6 -> 15, of which waited for: 6 -> 15; matrix products, arithmetic and copies ran while one was open for 0% -> 0% of each run, Pallas kernels for 0% -> 0%
where the time goes in v1:
time: 1050 us
  waiting for transfers between devices  830 us (79%)
  matrix products  77.2 us (7%)
  blocking collectives  57.8 us (6%)
  starting transfers between devices  40.9 us (4%)
  between operations  16.2 us (2%)
  local copies, waits for them, and re-layouts  14 us (1%)
  other arithmetic  11.6 us (1%)
    ppermute x12, waiting for transfers between devices, hamiltonian(): lax.ppermute(whole_sums, 'sec', [(dev, dev ^ hop) for dev in range(16)])  690 us
    all_gather x3, waiting for transfers between devices, hamiltonian(): gathered = lax.all_gather(iterate, 'op', axis=1, tiled=True)  140 us
    all_to_all x3, blocking collectives, hamiltonian(): lax.all_to_all(split_rows, 'op', split_axis=0, concat_axis=0, tiled=True)  57.8 us
    dot_general x3, matrix products, hamiltonian(): jnp.einsum('pmk,pnk->mn', left_product, right_ops, precision=highest)  41.4 us
    ppermute x12, starting transfers between devices, hamiltonian(): lax.ppermute(whole_sums, 'sec', [(dev, dev ^ hop) for dev in range(16)])  40.7 us
    dot_general x3, matrix products, hamiltonian(): jnp.einsum('pmr,rn->pmn', left_ops, chosen, precision=highest)  31.1 us
  transfers between devices with their start and end apart: 15, of which 15 were waited for; matrix products, arithmetic and copies ran while one was open for 0% of the time, Pallas kernels for 0%

profile of v1, /device:TPU:1, one launch (start us, length us, event | category | flops | bytes accessed | tf_op | source)
XLA Modules:
  0.0 1048.0 jit_solution(14944196980539690806)
XLA Ops:
  13.7 50.3 %all-gather.4.cloned.1.call-done = f32[2,512,512]{2,0,1:T(2,128)} async-done(((f32[2,32,512]{2,0,1:T(2,128)}), f32[2,512,512]{2,0,1:T(2,128)}) %all-gather.4.cloned.1.call-update) | async-done | bytes 2097168 | tf_op jit(solution)/shard_map/all_gather | solution.py:32
  63.9 2.5 constant_dynamic-slice_fusion.2
  67.8 10.5 %fusion.19 = f32[512,4,512]{2,0,1:T(8,128)S(1)} fusion(f32[4,512,512]{2,1,0:T(8,128)} %param.10, f32[1,512,512]{1,2,0:T(8,128)S(1)} %copy.18), kind=kOutput, calls=%fused_computation.19 | convolution fusion | flops 6442450944 | bytes 9437184 | tf_op jit(solution)/shard_map/pmr,rn->pmn/dot_general | solution.py:34
  78.3 13.7 %fusion.4 = f32[512,512,1]{1,0,2:T(8,128)S(1)} fusion(f32[4,512,512]{2,1,0:T(8,128)S(1)} %copy-done, f32[512,4,512]{2,0,1:T(8,128)S(1)} %fusion.19), kind=kOutput, calls=%fused_computation.4 | convolution fusion | flops 6442450944 | bytes 9437184 | tf_op jit(solution)/shard_map/pmk,pnk->mn/dot_general | solution.py:35
  92.1 19.3 %all_to_all.15 = f32[16,32,512]{2,1,0:T(8,128)S(1)} all-to-all(f32[16,32,512]{2,1,0:T(8,128)S(1)} %bitcast.75), channel_id=1, replica_groups=mesh['sec'=16,'op'=16] {'op'}, dimensions={0} | all-to-all | bytes 2097152 | tf_op jit(solution)/shard_map/all_to_all | solution.py:37
  112.9 3.3 collective-permute-start
  116.2 3.8 collective-permute-done
  122.0 45.6 %collective-permute-done.1 = f32[32,32,512]{2,0,1:T(8,128)S(1)} collective-permute-done((f32[32,32,512]{2,0,1:T(8,128)S(1)}, f32[32,32,512]{2,0,1:T(8,128)S(1)}, u32[]{:S(2)}, u32[]{:S(2)}) %collective-permute-start.1) | collective-permute-done | bytes 2097184 | tf_op jit(solution)/shard_map/ppermute | solution.py:45
  170.6 90.1 %collective-permute-done.2 = f32[32,32,512]{2,0,1:T(8,128)S(1)} collective-permute-done((f32[32,32,512]{2,0,1:T(8,128)S(1)}, f32[32,32,512]{2,0,1:T(8,128)S(1)}, u32[]{:S(2)}, u32[]{:S(2)}) %collective-permute-start.2) | collective-permute-done | bytes 2097184 | tf_op jit(solution)/shard_map/ppermute | solution.py:45
  261.1 6.5 collective-permute-start.3
  267.6 90.8 %collective-permute-done.3 = f32[32,32,512]{2,0,1:T(8,128)} collective-permute-done((f32[32,32,512]{2,0,1:T(8,128)S(1)}, f32[32,32,512]{2,0,1:T(8,128)}, u32[]{:S(2)}, u32[]{:S(2)}) %collective-permute-start.3) | collective-permute-done | bytes 2097184 | tf_op jit(solution)/shard_map/ppermute | solution.py:45
  360.4 45.1 %all-gather.6.cloned.1.call-done = f32[2,512,512]{2,0,1:T(2,128)} async-done(((f32[2,32,512]{2,0,1:T(2,128)}), f32[2,512,512]{2,0,1:T(2,128)}) %all-gather.6.cloned.1.call-update) | async-done | bytes 2097168 | tf_op jit(solution)/shard_map/all_gather | solution.py:32
  405.5 2.5 constant_dynamic-slice_fusion.1
  409.3 10.3 fusion.17
  419.6 13.9 %fusion.2 = f32[512,512,1]{1,0,2:T(8,128)S(1)} fusion(f32[4,512,512]{2,1,0:T(8,128)S(1)} %copy-done.1, f32[512,4,512]{2,0,1:T(8,128)S(1)} %fusion.17), kind=kOutput, calls=%fused_computation.2 | convolution fusion | flops 6442450944 | bytes 9437184 | tf_op jit(solution)/shard_map/pmk,pnk->mn/dot_general | solution.py:35
  433.5 19.3 %all_to_all.16 = f32[16,32,512]{2,1,0:T(8,128)S(1)} all-to-all(f32[16,32,512]{2,1,0:T(8,128)S(1)} %bitcast.76), channel_id=1, replica_groups=mesh['sec'=16,'op'=16] {'op'}, dimensions={0} | all-to-all | bytes 2097152 | tf_op jit(solution)/shard_map/all_to_all | solution.py:37
  454.4 3.4 collective-permute-start.4
  457.7 3.8 collective-permute-done.4
  463.5 45.6 %collective-permute-done.5 = f32[32,32,512]{2,0,1:T(8,128)S(1)} collective-permute-done((f32[32,32,512]{2,0,1:T(8,128)S(1)}, f32[32,32,512]{2,0,1:T(8,128)S(1)}, u32[]{:S(2)}, u32[]{:S(2)}) %collective-permute-start.5) | collective-permute-done | bytes 2097184 | tf_op jit(solution)/shard_map/ppermute | solution.py:45
  512.1 90.1 %collective-permute-done.6 = f32[32,32,512]{2,0,1:T(8,128)S(1)} collective-permute-done((f32[32,32,512]{2,0,1:T(8,128)S(1)}, f32[32,32,512]{2,0,1:T(8,128)S(1)}, u32[]{:S(2)}, u32[]{:S(2)}) %collective-permute-start.6) | collective-permute-done | bytes 2097184 | tf_op jit(solution)/shard_map/ppermute | solution.py:45
  602.8 6.5 collective-permute-start.7
  609.3 90.7 %collective-permute-done.7 = f32[32,32,512]{2,0,1:T(8,128)S(1)} collective-permute-done((f32[32,32,512]{2,0,1:T(8,128)S(1)}, f32[32,32,512]{2,0,1:T(8,128)S(1)}, u32[]{:S(2)}, u32[]{:S(2)}) %collective-permute-start.7) | collective-permute-done | bytes 2097184 | tf_op jit(solution)/shard_map/ppermute | solution.py:45
  701.0 45.1 %all-gather.8.cloned.1.call-done = f32[2,512,512]{2,0,1:T(2,128)} async-done(((f32[2,32,512]{2,0,1:T(2,128)}), f32[2,512,512]{2,0,1:T(2,128)}) %all-gather.8.cloned.1.call-update) | async-done | bytes 2097168 | tf_op jit(solution)/shard_map/all_gather | solution.py:32
  749.9 10.2 fusion.15
  760.2 13.7 %fusion = f32[512,512,1]{1,0,2:T(8,128)S(1)} fusion(f32[4,512,512]{2,1,0:T(8,128)S(1)} %copy-done.2, f32[512,4,512]{2,0,1:T(8,128)S(1)} %fusion.15), kind=kOutput, calls=%fused_computation | convolution fusion | flops 6442450944 | bytes 9437184 | tf_op jit(solution)/shard_map/pmk,pnk->mn/dot_general | solution.py:35
  773.9 19.3 %all_to_all.17 = f32[16,32,512]{2,1,0:T(8,128)S(1)} all-to-all(f32[16,32,512]{2,1,0:T(8,128)S(1)} %bitcast.77), channel_id=1, replica_groups=mesh['sec'=16,'op'=16] {'op'}, dimensions={0} | all-to-all | bytes 2097152 | tf_op jit(solution)/shard_map/all_to_all | solution.py:37
  794.7 3.3 collective-permute-start.8
  798.1 3.8 collective-permute-done.8
  803.9 45.6 %collective-permute-done.9 = f32[32,32,512]{2,0,1:T(8,128)S(1)} collective-permute-done((f32[32,32,512]{2,0,1:T(8,128)S(1)}, f32[32,32,512]{2,0,1:T(8,128)S(1)}, u32[]{:S(2)}, u32[]{:S(2)}) %collective-permute-start.9) | collective-permute-done | bytes 2097184 | tf_op jit(solution)/shard_map/ppermute | solution.py:45
  852.4 90.1 %collective-permute-done.10 = f32[32,32,512]{2,0,1:T(8,128)S(1)} collective-permute-done((f32[32,32,512]{2,0,1:T(8,128)S(1)}, f32[32,32,512]{2,0,1:T(8,128)S(1)}, u32[]{:S(2)}, u32[]{:S(2)}) %collective-permute-start.10) | collective-permute-done | bytes 2097184 | tf_op jit(solution)/shard_map/ppermute | solution.py:45
  943.1 6.5 collective-permute-start.11
  950.3 90.0 %collective-permute-done.11 = f32[32,32,512]{2,0,1:T(8,128)S(1)} collective-permute-done((f32[32,32,512]{2,0,1:T(8,128)S(1)}, f32[32,32,512]{2,0,1:T(8,128)S(1)}, u32[]{:S(2)}, u32[]{:S(2)}) %collective-permute-start.11) | collective-permute-done | bytes 2097184 | tf_op jit(solution)/shard_map/ppermute | solution.py:45
  (52 shorter events, 36.7 us)
Async XLA Ops:
  7.2 56.8 %all-gather.4.cloned.1.call-start = ((), (), s32[]{:S(2)}) async-start(), calls=%async_computation.3 | async-start | bytes 2228224 | tf_op jit(solution)/shard_map/all_gather | solution.py:32
  10.4 395.0 %all-gather.6.cloned.1.call-start = ((), (), s32[]{:S(2)}) async-start(), calls=%async_computation.4 | async-start | bytes 2228224 | tf_op jit(solution)/shard_map/all_gather | solution.py:32
  67.8 10.6 %copy-start = (f32[4,512,512]{2,1,0:T(8,128)S(1)}, f32[4,512,512]{2,1,0:T(8,128)}, u32[]{:S(2)}) copy-start(f32[4,512,512]{2,1,0:T(8,128)} %param.11) | copy-start | bytes 12582916
  92.0 19.3 %copy-start.6 = (s32[16]{0:T(128)S(1)}, s32[16]{0:T(128)}, u32[]{:S(2)}) copy-start(s32[16]{0:T(128)} %param.9) | copy-start | bytes 196
  112.9 7.1 collective-permute-start
  120.7 46.9 %collective-permute-start.1 = (f32[32,32,512]{2,0,1:T(8,128)S(1)}, f32[32,32,512]{2,0,1:T(8,128)S(1)}, u32[]{:S(2)}, u32[]{:S(2)}) collective-permute-start(f32[32,32,512]{2,0,1:T(8,128)S(1)} %add.65), channel_id=1, source_target_pairs={{0,32},{16,48},{32,0},{48,16},{64,96},{80,112},{96,64},{112,80},{1... | collective-permute-start | bytes 6291464 | tf_op jit(solution)/shard_map/ppermute | solution.py:45
  168.2 92.4 %collective-permute-start.2 = (f32[32,32,512]{2,0,1:T(8,128)S(1)}, f32[32,32,512]{2,0,1:T(8,128)S(1)}, u32[]{:S(2)}, u32[]{:S(2)}) collective-permute-start(f32[32,32,512]{2,0,1:T(8,128)S(1)} %add.66), channel_id=1, source_target_pairs={{0,64},{16,80},{32,96},{48,112},{64,0},{80,16},{96,32},{112,48},{1... | collective-permute-start | bytes 6291464 | tf_op jit(solution)/shard_map/ppermute | solution.py:45
  261.1 97.3 %collective-permute-start.3 = (f32[32,32,512]{2,0,1:T(8,128)S(1)}, f32[32,32,512]{2,0,1:T(8,128)}, u32[]{:S(2)}, u32[]{:S(2)}) collective-permute-start(f32[32,32,512]{2,0,1:T(8,128)S(1)} %add.67), channel_id=1, source_target_pairs={{0,128},{16,144},{32,160},{48,176},{64,192},{80,208},{96,224},{112... | collective-permute-start | bytes 6291464 | tf_op jit(solution)/shard_map/ppermute | solution.py:45
  360.3 385.7 %all-gather.8.cloned.1.call-start = ((), (), s32[]{:S(2)}) async-start(), calls=%async_computation.5 | async-start | bytes 2228224 | tf_op jit(solution)/shard_map/all_gather | solution.py:32
  409.3 10.3 copy-start.1
  454.4 7.1 collective-permute-start.4
  462.1 46.9 %collective-permute-start.5 = (f32[32,32,512]{2,0,1:T(8,128)S(1)}, f32[32,32,512]{2,0,1:T(8,128)S(1)}, u32[]{:S(2)}, u32[]{:S(2)}) collective-permute-start(f32[32,32,512]{2,0,1:T(8,128)S(1)} %add.70), channel_id=1, source_target_pairs={{0,32},{16,48},{32,0},{48,16},{64,96},{80,112},{96,64},{112,80},{1... | collective-permute-start | bytes 6291464 | tf_op jit(solution)/shard_map/ppermute | solution.py:45
  509.7 190.3 %copy-start.5 = (f32[2,32,512]{2,1,0:T(8,128)S(1)}, f32[2,32,512]{2,1,0:T(8,128)}, u32[]{:S(2)}) copy-start(f32[2,32,512]{2,1,0:T(8,128)} %param.6) | copy-start | bytes 393220
  509.7 92.4 %collective-permute-start.6 = (f32[32,32,512]{2,0,1:T(8,128)S(1)}, f32[32,32,512]{2,0,1:T(8,128)S(1)}, u32[]{:S(2)}, u32[]{:S(2)}) collective-permute-start(f32[32,32,512]{2,0,1:T(8,128)S(1)} %add.71), channel_id=1, source_target_pairs={{0,64},{16,80},{32,96},{48,112},{64,0},{80,16},{96,32},{112,48},{1... | collective-permute-start | bytes 6291464 | tf_op jit(solution)/shard_map/ppermute | solution.py:45
  602.8 97.3 %collective-permute-start.7 = (f32[32,32,512]{2,0,1:T(8,128)S(1)}, f32[32,32,512]{2,0,1:T(8,128)S(1)}, u32[]{:S(2)}, u32[]{:S(2)}) collective-permute-start(f32[32,32,512]{2,0,1:T(8,128)S(1)} %add.72), channel_id=1, source_target_pairs={{0,128},{16,144},{32,160},{48,176},{64,192},{80,208},{96,224},{112... | collective-permute-start | bytes 6291464 | tf_op jit(solution)/shard_map/ppermute | solution.py:45
  749.9 10.3 copy-start.2
  794.7 7.1 collective-permute-start.8
  802.5 46.9 %collective-permute-start.9 = (f32[32,32,512]{2,0,1:T(8,128)S(1)}, f32[32,32,512]{2,0,1:T(8,128)S(1)}, u32[]{:S(2)}, u32[]{:S(2)}) collective-permute-start(f32[32,32,512]{2,0,1:T(8,128)S(1)} %add.74), channel_id=1, source_target_pairs={{0,32},{16,48},{32,0},{48,16},{64,96},{80,112},{96,64},{112,80},{1... | collective-permute-start | bytes 6291464 | tf_op jit(solution)/shard_map/ppermute | solution.py:45
  850.1 99.6 %copy-start.4 = (f32[2,32,512]{2,0,1:T(2,128)S(1)}, f32[2,32,512]{2,0,1:T(2,128)}, u32[]{:S(2)}) copy-start(f32[2,32,512]{2,0,1:T(2,128)} %fusion.22) | copy-start | bytes 393220
  850.1 190.3 %copy-start.3 = (f32[2,32,512]{2,0,1:T(2,128)S(1)}, f32[2,32,512]{2,0,1:T(2,128)}, u32[]{:S(2)}) copy-start(f32[2,32,512]{2,0,1:T(2,128)} %and_select_fusion.2) | copy-start | bytes 393220
  850.1 92.4 %collective-permute-start.10 = (f32[32,32,512]{2,0,1:T(8,128)S(1)}, f32[32,32,512]{2,0,1:T(8,128)S(1)}, u32[]{:S(2)}, u32[]{:S(2)}) collective-permute-start(f32[32,32,512]{2,0,1:T(8,128)S(1)} %add.75), channel_id=1, source_target_pairs={{0,64},{16,80},{32,96},{48,112},{64,0},{80,16},{96,32},{112,48},{1... | collective-permute-start | bytes 6291464 | tf_op jit(solution)/shard_map/ppermute | solution.py:45
  943.1 97.2 %collective-permute-start.11 = (f32[32,32,512]{2,0,1:T(8,128)S(1)}, f32[32,32,512]{2,0,1:T(8,128)S(1)}, u32[]{:S(2)}, u32[]{:S(2)}) collective-permute-start(f32[32,32,512]{2,0,1:T(8,128)S(1)} %add.76), channel_id=1, source_target_pairs={{0,128},{16,144},{32,160},{48,176},{64,192},{80,208},{96,224},{112... | collective-permute-start | bytes 6291464 | tf_op jit(solution)/shard_map/ppermute | solution.py:45
Sparse Core Ops, SparseCore 0:
  11.0 52.8 all-gather.3
  360.5 44.9 all-gather.5
  701.1 44.9 all-gather.7
